TPU v7x, 256 devices: a whole 4x4x8 slice. The times are simulated.
256 devices in a mesh: dom: 256 (over x, z, y, core).
Axes of the slice: x: 4, y: 4, z: 8, core: 2. Of those that a mesh axis runs over, the one named last changes fastest.
Arguments:
- dof_state: float32 [9, 56, 229376], P(None, None, 'dom'), may hold values from -6 to 6
- jacobian_inv: float32 [3, 3, 229376], P(None, None, 'dom'), may hold values from -3.5 to 3.5
- face_normals: float32 [4, 3, 229376], P(None, None, 'dom'), may hold values from -3 to 3
- material: float32 [3, 229376], P(None, 'dom'), may hold values from 0.3 to 4.5, as said below
- deriv_mats: float32 [3, 35, 56], replicated, may hold values from -0.75 to 0.75
- stiff_mats: float32 [3, 56, 56], replicated, may hold values from -0.75 to 0.75
- trace_mats: float32 [4, 21, 56], replicated, may hold values from -0.75 to 0.75
- lift_mats: float32 [4, 56, 21], replicated, may hold values from -1.25 to 1.25
- orient_mats: float32 [3, 21, 21], replicated, may hold values from -1.25 to 1.25
- nbr_slot: int32 [4, 229376], P(None, 'dom'), may hold values from 0 to 1279, as said below
- nbr_face: int32 [4, 229376], P(None, 'dom'), may hold values from 0 to 3, as said below
- orient_code: int32 [4, 229376], P(None, 'dom'), may hold values from 0 to 2
- send_list: int32 [4, 3, 8192], P(None, None, 'dom'), may hold values from -1 to 3583, as said below
Outputs:
- new_state: float32 [9, 56, 229376], P(None, None, 'dom')
Inputs may be any that keep to these rules, and one draw needn't show every extreme that they name: `send_list`: entry [p, c, d * 32 + k] is what device d sends as slot k of its list for peer p (device d + offset_p with offsets -2, -1, +1, +2, wrapping) and receiving cluster c: sender element * 4 + face, live entries first, then -1. `nbr_slot`: below 896: a local element. Else 896 + (p * 3 + c) * 32 + k: live slot k of the list that device (own - offset_p) sends for peer p and cluster c, where c is this element's cluster; every live slot is named by exactly one face. `nbr_face`: for a face that names a slot, the face stored in that slot's entry. `material`: rows are density, first Lame parameter, shear modulus.
All inputs are finite; a program needn't handle non-finite values.
Results may differ from a plain program's by a relative error of at most 0.0003.
Values sent between devices are 32-bit elements; how exact they have to be, the bound alone decides.
A program may use at most 192 MiB of HBM per device.

v0:
```python
import math

import jax
import jax.numpy as jnp
from jax import lax
from jax.experimental import pallas as pl
from jax.experimental.pallas import tpu as pltpu
from jax.sharding import PartitionSpec as P

NQ = 9
NB = 56
NF = 21
FR = 24
LANE = 128
TILES = 7
PEERS = 4
CAPC = 32
ELEMS = TILES * LANE
F32 = jnp.float32
BF16 = jnp.bfloat16

step_size = 0.04
peer_offsets = (-2, -1, 1, 2)
level_rows = (56, 40, 24, 16, 8, 8)
level_k = (64, 48, 32, 16, 16)
level_m = (128, 80, 48, 32, 32)
sizes = (56, 35, 20, 10, 4, 1)
STIFF_M = 272
ROWS = NQ * FR
PACK = 56


def time_weights(lower, upper):
    return [
        step_size ** (k + 1) * (upper ** (k + 1) - lower ** (k + 1)) / math.factorial(k + 1)
        for k in range(6)
    ]


def split3(a):
    hi = lax.reduce_precision(a, 8, 7)
    lo = lax.reduce_precision(a - hi, 8, 7)
    return jnp.concatenate([hi, hi, lo], axis=1).astype(BF16)


def pad2(a, rows, cols):
    return jnp.pad(a, ((0, rows - a.shape[0]), (0, cols - a.shape[1])))


def prepare(deriv_mats, stiff_mats, trace_mats, lift_mats, orient_mats):
    mats = []
    for k in range(5):
        n_in, n_out = sizes[k], sizes[k + 1]
        blocks = [
            pad2(deriv_mats[xi, :n_out, :n_in], level_rows[k + 1], level_k[k]) for xi in range(3)
        ]
        mats.append(split3(pad2(jnp.concatenate(blocks, axis=0), level_m[k], level_k[k])))
    trace = jnp.concatenate([pad2(trace_mats[f], FR, 64) for f in range(4)], axis=0)
    stiff = pad2(stiff_mats.reshape(3 * NB, NB), 3 * NB, 64)
    mats.append(split3(pad2(jnp.concatenate([stiff, trace], axis=0), STIFF_M, 64)))
    mats.append(split3(trace))
    turn = jnp.concatenate([pad2(orient_mats[h], FR, 32) for h in range(3)], axis=0)
    mats.append(split3(pad2(turn, 80, 32)))
    lift = jnp.concatenate([pad2(lift_mats[f], 64, FR) for f in range(4)], axis=1)
    mats.append(split3(lift))
    return mats


def hi_lo(x):
    hi = x.astype(BF16)
    return hi, (x - hi.astype(F32)).astype(BF16)


def kernel(
    n_dev,
    top_ref,
    state_in,
    jac_ref,
    nrm_ref,
    mat_ref,
    m0,
    m1,
    m2,
    m3,
    m4,
    m_stiff,
    m_trace,
    m_orient,
    m_lift,
    slot_ref,
    face_ref,
    code_ref,
    send_ref,
    out_ref,
    coef,
    tabs,
    onehot,
    onehot_send,
    onehot_ghost,
    meta,
    meta_send,
    own,
    seen,
    gath,
    der,
    x3,
    lv1,
    lv2,
    lv3,
    lv4,
    lv5,
    acc,
    fl,
    x_lift,
    ghost,
    sbuf,
    rbuf,
    send_sem,
    recv_sem,
):
    me = lax.axis_index("dom")
    targets = [lax.rem(me + n_dev + off, n_dev) for off in peer_offsets]
    level_mats = (m0, m1, m2, m3, m4)
    level_refs = (None, lv1, lv2, lv3, lv4, lv5)
    barrier = pltpu.get_barrier_semaphore()
    for dev in targets:
        pl.semaphore_signal(barrier, inc=1, device_id=(dev,), device_id_type=pl.DeviceIdType.MESH)

    half_top = 0.5 * top_ref[0, 0]
    out_ref[...] = state_in[...]
    mat = mat_ref[...]
    inv_rho = 1.0 / mat[0:1]
    rows = [jac_ref[xi][j : j + 1] for xi in range(3) for j in range(3)]
    rows += [nrm_ref[f][j : j + 1] for f in range(4) for j in range(3)]
    rows += [mat[1:2], 2.0 * mat[2:3], mat[2:3], inv_rho]
    for t in range(TILES):
        for i, row in enumerate(rows):
            coef[t, i] = jnp.broadcast_to(row[:, t * LANE : (t + 1) * LANE], (8, LANE))

    slots = slot_ref[...]
    faces = face_ref[...]
    codes = code_ref[...]
    away = slots - ELEMS
    peer = (
        (away >= 96).astype(jnp.int32)
        + (away >= 192).astype(jnp.int32)
        + (away >= 288).astype(jnp.int32)
    )
    ghost_col = jnp.where(away >= 0, peer * CAPC + (away & (CAPC - 1)), -1)
    elem_rows = lax.broadcasted_iota(jnp.int32, (ELEMS, LANE), 0)
    ghost_rows = lax.broadcasted_iota(jnp.int32, (LANE, LANE), 0)

    def hot(rows_iota, line):
        return jnp.where(rows_iota == line, 1.0, 0.0).astype(BF16)

    for t in range(TILES):
        for f in range(4):
            cut = slice(t * LANE, (t + 1) * LANE)
            at = slice(f * LANE, (f + 1) * LANE)
            onehot[t, :, at] = hot(elem_rows, slots[f : f + 1, cut])
            g = hot(ghost_rows, ghost_col[f : f + 1, cut])
            onehot_ghost[t, 0:LANE, at] = g
            onehot_ghost[t, LANE : 2 * LANE, at] = g
            meta[t, 0, :, at] = jnp.broadcast_to(faces[f : f + 1, cut], (8, LANE))
            meta[t, 1, :, at] = jnp.broadcast_to(codes[f : f + 1, cut], (8, LANE))
    sends = send_ref[...]
    send_elem = jnp.where(sends >= 0, sends >> 2, -1)
    send_face = sends & 3
    for c in range(3):
        onehot_send[c] = hot(elem_rows, send_elem[c : c + 1])
        meta_send[c] = jnp.broadcast_to(send_face[c : c + 1], (8, LANE))

    pl.semaphore_wait(barrier, PEERS)


    def star_rows(c, read):
        n_xi = len(c)

        def total(pairs):
            out = None
            for xi in range(n_xi):
                for j, q in pairs:
                    term = c[xi][j] * vals[xi][q]
                    out = term if out is None else out + term
            return out

        vals = [[read(xi, q) for q in range(NQ)] for xi in range(n_xi)]
        return total

    def star(c, lam, mu2, mu, irho, read):
        total = star_rows(c, read)
        p = total([(0, 6)])
        q = total([(1, 7)])
        r = total([(2, 8)])
        div = lam * (p + q + r)
        return [
            div + mu2 * p,
            div + mu2 * q,
            div + mu2 * r,
            mu * total([(1, 6), (0, 7)]),
            mu * total([(2, 7), (1, 8)]),
            mu * total([(2, 6), (0, 8)]),
            irho * total([(0, 0), (1, 3), (2, 5)]),
            irho * total([(0, 3), (1, 1), (2, 4)]),
            irho * total([(0, 5), (1, 4), (2, 2)]),
        ]

    def store_split(ref, row, col, k_pad, x, width):
        hi, lo = hi_lo(x)
        ref[row : row + 16, col : col + width] = hi
        ref[k_pad + row : k_pad + row + 16, col : col + width] = lo
        ref[2 * k_pad + row : 2 * k_pad + row + 16, col : col + width] = hi

    def put_operand(ref, k_pad, q, pieces):
        if len(pieces) % 2:
            pieces = pieces + [jnp.zeros((8, LANE), F32)]
        for i in range(0, len(pieces), 2):
            pair = jnp.concatenate([pieces[i], pieces[i + 1]], axis=0)
            store_split(ref, i * 8, q * LANE, k_pad, pair, LANE)

    def predict(tile, table_of, weights):
        base = pl.multiple_of(tile * LANE, LANE)
        lanes = pl.ds(base, LANE)
        cj = [[coef[tile, 3 * xi + j] for j in range(3)] for xi in range(3)]
        lam, mu2, mu, irho = [coef[tile, 21 + i] for i in range(4)]
        for q in range(NQ):
            put_operand(x3, 64, q, [out_ref[q, r * 8 : r * 8 + 8, lanes] for r in range(7)])
        for k in range(5):
            kp = level_k[k]
            m = level_m[k]
            der[0:m, :] = jnp.dot(
                level_mats[k][...], x3[0 : 3 * kp, :], preferred_element_type=F32
            )
            n = level_rows[k + 1]
            pend = [[] for _ in range(NQ)]
            for r in range(n // 8):

                def read(xi, q, r=r):
                    lo_row = xi * n + r * 8
                    return der[lo_row : lo_row + 8, q * LANE : (q + 1) * LANE]

                vals = star(cj, lam, mu2, mu, irho, read)
                for q in range(NQ):
                    level_refs[k + 1][q, r * 8 : r * 8 + 8, :] = vals[q]
                    pend[q].append(vals[q])
                last = r == n // 8 - 1
                if k < 4 and (r % 2 == 1 or last):
                    for q in range(NQ):
                        lo_piece = pend[q][0]
                        hi_piece = pend[q][1] if len(pend[q]) == 2 else jnp.zeros((8, LANE), F32)
                        pair = jnp.concatenate([lo_piece, hi_piece], axis=0)
                        store_split(x3, (r // 2) * 16, q * LANE, level_k[k + 1], pair, LANE)
                if r % 2 == 1 or last:
                    pend = [[] for _ in range(NQ)]
        own_pend = [[] for _ in range(NQ)]
        held = {}
        for v in range(64):
            if v < 63:
                q, r = divmod(v, 7)
                terms = [out_ref[q, r * 8 : r * 8 + 8, lanes]]
                for k in range(1, 6):
                    if r * 8 < level_rows[k]:
                        terms.append(level_refs[k][q, r * 8 : r * 8 + 8, :])
                ticks = []
                for w in weights:
                    total = terms[0] * w[0]
                    for k in range(1, len(terms)):
                        total = total + terms[k] * w[k]
                    ticks.append(total)
                entries, own_int = table_of(v, ticks)
                own_pend[q].append(own_int)
                if r == 6:
                    put_operand(x3, 64, q, own_pend[q])
            else:
                entries = [(idx, jnp.zeros((8, LANE), F32)) for idx, _ in entries]
            if v % 2 == 0:
                held = entries
            else:
                for (idx, first), (_, second) in zip(held, entries):
                    hi, lo = hi_lo(jnp.concatenate([first, second], axis=0))
                    row = (v // 2) * 16
                    tabs[idx, row : row + 16, lanes] = hi
                    tabs[idx, 512 + row : 512 + row + 16, lanes] = lo
        der[...] = jnp.dot(m_stiff[...], x3[...], preferred_element_type=F32)
        for r in range(7):

            def read(xi, q, r=r):
                lo_row = xi * NB + r * 8
                return der[lo_row : lo_row + 8, q * LANE : (q + 1) * LANE]

            vals = star(cj, lam, mu2, mu, irho, read)
            for q in range(NQ):
                out_ref[q, r * 8 : r * 8 + 8, lanes] = (
                    out_ref[q, r * 8 : r * 8 + 8, lanes] - vals[q]
                )
        own[tile] = der[168 : 168 + 96, :]

    def gather_traces(table, hot_mat, face_rows, width, put):
        gath[:, 0:width] = jnp.dot(tabs[table], hot_mat, preferred_element_type=F32)
        is_one, is_two, is_three = [
            jnp.concatenate([face_rows == i] * 3, axis=0) for i in (1, 2, 3)
        ]
        zero = jnp.zeros((8, width), F32)
        for q in range(NQ):
            hi = jnp.concatenate([gath[q * NB : (q + 1) * NB, 0:width], zero], axis=0).astype(BF16)
            lo = jnp.concatenate(
                [gath[512 + q * NB : 512 + (q + 1) * NB, 0:width], zero], axis=0
            ).astype(BF16)
            x = jnp.concatenate([hi, lo, hi], axis=0)
            t = jnp.dot(m_trace[...], x, preferred_element_type=F32)
            pick = jnp.where(
                is_three,
                t[3 * FR : 4 * FR],
                jnp.where(
                    is_two, t[2 * FR : 3 * FR], jnp.where(is_one, t[FR : 2 * FR], t[0:FR])
                ),
            )
            put(q, pick)

    lane_group = lax.broadcasted_iota(jnp.int32, (PACK, LANE), 1) // CAPC

    def transpose_blocks(read):
        outs = []
        blocks = [read(g) for g in range(4)]
        for p in range(4):
            out = None
            for g in range(4):
                shift = ((g - p) * CAPC) % LANE
                turned = pltpu.roll(blocks[g], shift, 1) if shift else blocks[g]
                out = turned if out is None else jnp.where(lane_group == g, turned, out)
            outs.append(out)
        return outs

    def copies(combo):
        return [
            pltpu.make_async_remote_copy(
                src_ref=sbuf.at[combo, p],
                dst_ref=rbuf.at[combo, p],
                send_sem=send_sem.at[combo, p],
                recv_sem=recv_sem.at[combo, p],
                device_id=(targets[p],),
                device_id_type=pl.DeviceIdType.MESH,
            )
            for p in range(PEERS)
        ]

    def send_cluster(c, combo):
        def put(q, pick):
            ghost_stage[q * FR : (q + 1) * FR, :] = pick

        ghost_stage = fl.at[0 : 4 * PACK, 0:LANE]
        ghost_stage[ROWS : 4 * PACK, :] = jnp.zeros((4 * PACK - ROWS, LANE), F32)
        gather_traces(combo, onehot_send[c], meta_send[c], LANE, put)
        outs = transpose_blocks(lambda g: ghost_stage[g * PACK : (g + 1) * PACK, :])
        for p in range(PEERS):
            sbuf[combo, p] = outs[p]
        for copy in copies(combo):
            copy.start()

    def gather_tile(tile, table):
        def put(q, pick):
            seen[tile, q * FR : (q + 1) * FR, :] = pick

        gather_traces(table, onehot[tile], meta[tile, 0], 4 * LANE, put)

    def receive_cluster(c, combo):
        for copy in copies(combo):
            copy.wait()
        outs = transpose_blocks(lambda p: rbuf[combo, p])
        full = jnp.concatenate(outs, axis=0)
        hi, lo = hi_lo(full)
        ghost[c, :, 0:LANE] = hi
        ghost[c, :, LANE : 2 * LANE] = lo

    def correct_tile(tile, c):
        base = pl.multiple_of(tile * LANE, LANE)
        lanes = pl.ds(base, LANE)
        gath[0 : 4 * PACK, :] = jnp.dot(
            ghost[c], onehot_ghost[tile], preferred_element_type=F32
        )
        code = meta[tile, 1]
        is_one, is_two = [jnp.concatenate([code == i] * 3, axis=0) for i in (1, 2)]
        zero = jnp.zeros((8, 4 * LANE), F32)
        for q in range(NQ):
            cut = slice(q * FR, (q + 1) * FR)
            arrived = seen[tile, cut, :] + gath[cut, :]
            hi, lo = hi_lo(jnp.concatenate([arrived, zero], axis=0))
            x = jnp.concatenate([hi, lo, hi], axis=0)
            t = jnp.dot(m_orient[...], x, preferred_element_type=F32)
            seen[tile, cut, :] = jnp.where(
                is_two, t[2 * FR : 3 * FR], jnp.where(is_one, t[FR : 2 * FR], t[0:FR])
            )
        lam, mu2, mu, irho = [-0.5 * coef[tile, 21 + i] for i in range(4)]
        for f in range(4):
            normal = [[coef[tile, 9 + 3 * f + j] for j in range(3)]]
            for r in range(3):
                inner = [
                    own[tile, f * FR + r * 8 : f * FR + r * 8 + 8, q * LANE : (q + 1) * LANE]
                    for q in range(NQ)
                ]
                outer = [
                    seen[
                        tile, q * FR + r * 8 : q * FR + r * 8 + 8, f * LANE : (f + 1) * LANE
                    ]
                    for q in range(NQ)
                ]
                both = [a + b for a, b in zip(inner, outer)]
                vals = star(normal, lam, mu2, mu, irho, lambda xi, q: both[q])
                for q in range(NQ):
                    row = f * FR + r * 8
                    fl[row : row + 8, q * LANE : (q + 1) * LANE] = vals[q] + half_top * (
                        inner[q] - outer[q]
                    )
        for i in range(6):
            for q in range(NQ):
                col = q * LANE
                store_split(
                    x_lift, i * 16, col, 96, fl[i * 16 : i * 16 + 16, col : col + LANE], LANE
                )
        der[0:64, :] = jnp.dot(m_lift[...], x_lift[...], preferred_element_type=F32)
        for q in range(NQ):
            out_ref[q, :, lanes] = out_ref[q, :, lanes] - der[0:NB, q * LANE : (q + 1) * LANE]


    acc[...] = jnp.zeros_like(acc)
    w_tick = [time_weights(i, i + 1) for i in range(4)]

    def tables_2(v, ticks):
        j0, j1, j2, j3 = ticks
        first, second = j0 + j1, j2 + j3
        whole = first + second
        return [(0, j0), (1, j1), (2, j2), (3, j3), (4, first), (5, second), (6, whole)], whole

    def predict_2(i, carry):
        predict(3 + i, tables_2, w_tick)
        return carry

    lax.fori_loop(0, 4, predict_2, 0)

    def tick(t, carry):
        half = t // 2
        odd = t - 2 * half
        last = t // 3

        @pl.when(odd == 0)
        def _():
            def tables_1(v, ticks):
                j0, j1 = ticks
                pair = j0 + j1
                return [(t, j0), (t + 1, j1), (4 + half, pair)], pair

            def tables_1_all(i):
                def inner(v, ticks):
                    entries, pair = tables_1(v, ticks)
                    whole = pair + acc[2 + i, v * 8 : v * 8 + 8, :]
                    acc[2 + i, v * 8 : v * 8 + 8, :] = whole
                    return entries + [(6, whole)], pair

                return inner

            def predict_1(i, carry):
                predict(1 + i, tables_1_all(i), w_tick[:2])
                return carry

            lax.fori_loop(0, 2, predict_1, 0)

        keep = (1 - odd).astype(F32)

        def tables_0(v, ticks):
            (j0,) = ticks
            rows_v = slice(v * 8, v * 8 + 8)
            pair = j0 + acc[0, rows_v, :]
            acc[0, rows_v, :] = pair * keep
            whole = j0 + acc[1, rows_v, :]
            acc[1, rows_v, :] = whole
            return [(t, j0), (4 + half, pair), (6, whole)], j0

        predict(0, tables_0, w_tick[:1])

        n_due = 1 + odd + last
        n_tiles = 1 + 2 * odd + 4 * last

        def combo_of(a, b):
            return (1 - a) * t + (a - b) * (4 + half) + b * 6

        def send_step(c, carry):
            a = (c + 1) // 2
            b = c // 2
            send_cluster(c, combo_of(a, b))
            return carry

        def gather_step(j, carry):
            a = (j + 6) // 7
            b = (j + 4) // 7
            gather_tile(j, combo_of(a, b))
            return carry

        def receive_step(c, carry):
            a = (c + 1) // 2
            b = c // 2
            receive_cluster(c, combo_of(a, b))
            return carry

        def correct_step(j, carry):
            correct_tile(j, (j + 6) // 7 + (j + 4) // 7)
            return carry

        lax.fori_loop(0, n_due, send_step, 0)
        lax.fori_loop(0, n_tiles, gather_step, 0)
        lax.fori_loop(0, n_due, receive_step, 0)
        lax.fori_loop(0, n_tiles, correct_step, 0)
        return carry

    lax.fori_loop(0, 4, tick, 0)


def local(
    dof_state,
    jacobian_inv,
    face_normals,
    material,
    deriv_mats,
    stiff_mats,
    trace_mats,
    lift_mats,
    orient_mats,
    nbr_slot,
    nbr_face,
    orient_code,
    send_list,
):
    n_dev = lax.axis_size("dom")
    top = jnp.max(jnp.sqrt((material[1] + 2.0 * material[2]) * (1.0 / material[0])))
    top = lax.pmax(top, "dom").reshape(1, 1)
    mats = prepare(deriv_mats, stiff_mats, trace_mats, lift_mats, orient_mats)
    sends = jnp.transpose(send_list, (1, 0, 2)).reshape(3, LANE)
    vmem = pl.BlockSpec(memory_space=pltpu.VMEM)

    def run(*refs):
        kernel(n_dev, *refs)

    return pl.pallas_call(
        run,
        out_shape=jax.ShapeDtypeStruct((NQ, NB, ELEMS), F32),
        in_specs=[pl.BlockSpec(memory_space=pltpu.SMEM)] + [vmem] * 17,
        out_specs=vmem,
        scratch_shapes=[
            pltpu.VMEM((TILES, 25, 8, LANE), F32),
            pltpu.VMEM((7, 1024, ELEMS), BF16),
            pltpu.VMEM((TILES, ELEMS, 4 * LANE), BF16),
            pltpu.VMEM((3, ELEMS, LANE), BF16),
            pltpu.VMEM((TILES, 2 * LANE, 4 * LANE), BF16),
            pltpu.VMEM((TILES, 2, 8, 4 * LANE), jnp.int32),
            pltpu.VMEM((3, 8, LANE), jnp.int32),
            pltpu.VMEM((TILES, 96, NQ * LANE), F32),
            pltpu.VMEM((TILES, ROWS, 4 * LANE), F32),
            pltpu.VMEM((1024, 4 * LANE), F32),
            pltpu.VMEM((STIFF_M, NQ * LANE), F32),
            pltpu.VMEM((192, NQ * LANE), BF16),
            pltpu.VMEM((NQ, 40, LANE), F32),
            pltpu.VMEM((NQ, 24, LANE), F32),
            pltpu.VMEM((NQ, 16, LANE), F32),
            pltpu.VMEM((NQ, 8, LANE), F32),
            pltpu.VMEM((NQ, 8, LANE), F32),
            pltpu.VMEM((4, NQ * NB, LANE), F32),
            pltpu.VMEM((4 * PACK, NQ * LANE), F32),
            pltpu.VMEM((288, NQ * LANE), BF16),
            pltpu.VMEM((3, 4 * PACK, 2 * LANE), BF16),
            pltpu.VMEM((7, PEERS, PACK, LANE), F32),
            pltpu.VMEM((7, PEERS, PACK, LANE), F32),
            pltpu.SemaphoreType.DMA((7, PEERS)),
            pltpu.SemaphoreType.DMA((7, PEERS)),
        ],
        compiler_params=pltpu.CompilerParams(
            collective_id=0, has_side_effects=True, vmem_limit_bytes=58 * 1024 * 1024
        ),
        cost_estimate=pl.CostEstimate(
            flops=25_000_000_000, bytes_accessed=6_000_000, transcendentals=0
        ),
    )(
        top,
        dof_state,
        jacobian_inv,
        face_normals,
        material,
        *mats,
        nbr_slot,
        nbr_face,
        orient_code,
        sends,
    )


def solution(mesh):
    return jax.shard_map(
        local,
        mesh=mesh,
        in_specs=(
            P(None, None, "dom"),
            P(None, None, "dom"),
            P(None, None, "dom"),
            P(None, "dom"),
            P(),
            P(),
            P(),
            P(),
            P(),
            P(None, "dom"),
            P(None, "dom"),
            P(None, "dom"),
            P(None, None, "dom"),
        ),
        out_specs=P(None, None, "dom"),
        check_vma=False,
    )
```

profile of v0, /device:TPU:1, one launch (start us, length us, event | category | flops | bytes accessed | tf_op | source)
XLA Modules:
  0.0 175.1 jit_solution(2691065741860368840)
XLA Ops:
  0.0 0.0 copy-start
  0.0 0.0 copy-start.1
  0.0 0.0 copy-start.2
  0.0 1.5 sqrt_reduce_fusion
  1.5 81.4 %pmax.7.refs_0_ = f32[1,1]{1,0:T(1,128)} all-reduce(f32[1,1]{1,0:T(1,128)} %bitcast), channel_id=1, replica_groups=mesh['dom'=256] {'dom'}, use_global_device_ids=true, to_apply=%region_1.0 | all-reduce | flops 1 | bytes 8 | tf_op jit(solution)/shard_map/pmax | solution.py:534
  82.8 0.7 slice_bitcast_fusion.14
  83.6 1.3 reshape.18.refs_17_
  84.9 0.7 slice_bitcast_fusion.11
  85.6 0.7 pad_maximum_fusion.8
  86.3 0.7 slice_bitcast_fusion.8
  87.1 0.7 pad_maximum_fusion.7.refs_7_
  87.7 0.7 fusion.27
  88.5 0.1 copy.53
  88.6 0.1 copy.54
  88.7 0.1 copy.55
  88.8 0.1 select_maximum_fusion.9
  88.9 0.1 copy.43
  89.0 0.7 pad_maximum_fusion.6.refs_12_
  89.6 0.7 slice_bitcast_fusion.5
  90.4 0.7 pad_maximum_fusion.5.refs_6_
  91.1 1.0 fusion.26
  92.1 1.0 fusion.25
  93.1 0.1 copy.56
  93.2 0.1 copy.58
  93.3 0.1 copy.57
  93.4 0.1 copy.59
  93.5 0.1 reduce-precision_convert_fusion.5
  93.6 0.7 pad_maximum_fusion.4.refs_13_
  94.3 0.0 copy-done.2
  94.3 0.6 copy.48.refs_3_
  95.0 0.0 copy-done
  95.0 0.7 pad_maximum_fusion.1.refs_5_
  95.7 0.0 copy-done.1
  95.8 0.7 pad_maximum_fusion.3.refs_11_
  96.6 0.8 pad_maximum_fusion.refs_10_
  97.3 75.0 %shard_map.127 = f32[9,56,896]{2,1,0:T(8,128)} custom-call(f32[1,1]{1,0:T(1,128)} %pmax.7.refs_0_, f32[9,56,896]{2,1,0:T(8,128)} %refs_1_.1, f32[3,3,896]{2,1,0:T(4,128)} %refs_2_.1, f32[4,3,896]{2,1,0:T(4,128)} %copy.48.refs_3_, f32[3,896]{1,0:T(4,128)} %refs_4_.1, bf16[128,192]{1,0:T(8,128)(2,1)} %pad_maximum_fusion.1.refs_5_, ...), custom_call_target="tpu_custom_call" | custom-call | flops 24999999488 | bytes 6000000 | tf_op jit(solution)/shard_map/pallas_call | solution.py:542
  172.3 2.8 %copy.69 = f32[9,56,896]{2,1,0:T(8,128)} copy(f32[9,56,896]{2,1,0:T(8,128)} %shard_map.127) | data formatting | bytes 3612672
  (21 shorter events, 0.2 us)
Async XLA Ops:
  0.0 95.0 %copy-start = (f32[3,35,56]{2,1,0:T(8,128)S(1)}, f32[3,35,56]{2,1,0:T(8,128)}, u32[]{:S(2)}) copy-start(f32[3,35,56]{2,1,0:T(8,128)} %param.17) | copy-start | bytes 70564
  0.0 95.7 %copy-start.1 = (f32[3,56,56]{2,1,0:T(8,128)S(1)}, f32[3,56,56]{2,1,0:T(8,128)}, u32[]{:S(2)}) copy-start(f32[3,56,56]{2,1,0:T(8,128)} %param.18) | copy-start | bytes 112900
  0.0 94.3 %copy-start.2 = (f32[4,3,896]{2,0,1:T(4,128)S(1)}, f32[4,3,896]{2,0,1:T(4,128)}, u32[]{:S(2)}) copy-start(f32[4,3,896]{2,0,1:T(4,128)} %param.15) | copy-start | bytes 129028
where the time goes:
time: 176 us; the launch traced here: 175 us
  blocking collectives  81.4 us (46%)
  Pallas kernels  75 us (43%)
  local copies, waits for them, and re-layouts  11.2 us (6%)
  other arithmetic  7.45 us (4%)
    pmax x1, blocking collectives, local(): top = lax.pmax(top, 'dom').reshape(1, 1)  81.4 us
    pallas_call x1, Pallas kernels, local(): pl.pallas_call(run, out_shape=jax.ShapeDtypeStruct((NQ, NB, ELEMS), F32),...  75 us
    concatenate x8, other arithmetic, split3(): return jnp.concatenate([hi, hi, lo], axis=1).astype(BF16)  5.66 us
    unnamed x16, local copies, waits for them, and re-layouts  4.11 us

commit v1 on v0

--- a/solution.py
+++ b/solution.py
@@ -37,35 +37,6 @@
     ]
 
 
-def split3(a):
-    hi = lax.reduce_precision(a, 8, 7)
-    lo = lax.reduce_precision(a - hi, 8, 7)
-    return jnp.concatenate([hi, hi, lo], axis=1).astype(BF16)
-
-
-def pad2(a, rows, cols):
-    return jnp.pad(a, ((0, rows - a.shape[0]), (0, cols - a.shape[1])))
-
-
-def prepare(deriv_mats, stiff_mats, trace_mats, lift_mats, orient_mats):
-    mats = []
-    for k in range(5):
-        n_in, n_out = sizes[k], sizes[k + 1]
-        blocks = [
-            pad2(deriv_mats[xi, :n_out, :n_in], level_rows[k + 1], level_k[k]) for xi in range(3)
-        ]
-        mats.append(split3(pad2(jnp.concatenate(blocks, axis=0), level_m[k], level_k[k])))
-    trace = jnp.concatenate([pad2(trace_mats[f], FR, 64) for f in range(4)], axis=0)
-    stiff = pad2(stiff_mats.reshape(3 * NB, NB), 3 * NB, 64)
-    mats.append(split3(pad2(jnp.concatenate([stiff, trace], axis=0), STIFF_M, 64)))
-    mats.append(split3(trace))
-    turn = jnp.concatenate([pad2(orient_mats[h], FR, 32) for h in range(3)], axis=0)
-    mats.append(split3(pad2(turn, 80, 32)))
-    lift = jnp.concatenate([pad2(lift_mats[f], 64, FR) for f in range(4)], axis=1)
-    mats.append(split3(lift))
-    return mats
-
-
 def hi_lo(x):
     hi = x.astype(BF16)
     return hi, (x - hi.astype(F32)).astype(BF16)
@@ -73,11 +44,21 @@
 
 def kernel(
     n_dev,
-    top_ref,
+    radices,
     state_in,
     jac_ref,
     nrm_ref,
     mat_ref,
+    deriv_ref,
+    stiff_ref,
+    trace_ref,
+    lift_ref,
+    orient_ref,
+    slot_ref,
+    face_ref,
+    code_ref,
+    send_ref,
+    out_ref,
     m0,
     m1,
     m2,
@@ -87,11 +68,12 @@
     m_trace,
     m_orient,
     m_lift,
-    slot_ref,
-    face_ref,
-    code_ref,
-    send_ref,
-    out_ref,
+    stage,
+    send_stage,
+    top_out,
+    top_in,
+    top_send_sem,
+    top_recv_sem,
     coef,
     tabs,
     onehot,
@@ -122,16 +104,102 @@
     targets = [lax.rem(me + n_dev + off, n_dev) for off in peer_offsets]
     level_mats = (m0, m1, m2, m3, m4)
     level_refs = (None, lv1, lv2, lv3, lv4, lv5)
+    partners = []
+    stride = 1
+    for radix in radices:
+        place = lax.rem(me // stride, radix)
+        partners.append(
+            [me + (lax.rem(place + i, radix) - place) * stride for i in range(1, radix)]
+        )
+        stride *= radix
+    greeted = targets + [dev for group in partners for dev in group]
     barrier = pltpu.get_barrier_semaphore()
-    for dev in targets:
+    for dev in greeted:
         pl.semaphore_signal(barrier, inc=1, device_id=(dev,), device_id_type=pl.DeviceIdType.MESH)
 
-    half_top = 0.5 * top_ref[0, 0]
-    out_ref[...] = state_in[...]
     mat = mat_ref[...]
     inv_rho = 1.0 / mat[0:1]
+    speed = jnp.sqrt((mat[1:2] + 2.0 * mat[2:3]) * inv_rho)
+    top_out[0] = jnp.broadcast_to(jnp.max(speed, axis=1, keepdims=True), (8, LANE))
+
+    def top_copies(level):
+        return [
+            pltpu.make_async_remote_copy(
+                src_ref=top_out.at[level],
+                dst_ref=top_in.at[level, i],
+                send_sem=top_send_sem.at[level, i],
+                recv_sem=top_recv_sem.at[level, i],
+                device_id=(dev,),
+                device_id_type=pl.DeviceIdType.MESH,
+            )
+            for i, dev in enumerate(partners[level])
+        ]
+
+    def top_start(level):
+        for copy in top_copies(level):
+            copy.start()
+
+    def top_finish(level):
+        for copy in top_copies(level):
+            copy.wait()
+        best = top_out[level]
+        for i in range(len(partners[level])):
+            best = jnp.maximum(best, top_in[level, i])
+        top_out[level + 1] = best
+
+    n_levels = len(radices)
+    lane_of = lax.broadcasted_iota(jnp.int32, (stage.shape[0], LANE), 1)
+
+    def lay(m_ref, rows, k_pad, base):
+        hi = base.astype(BF16).astype(F32)
+        lo = base - hi
+        cols = [None] * (m_ref.shape[1] // LANE)
+        for i, part in enumerate((hi, hi, lo)):
+            at = i * k_pad
+            col, off = divmod(at, LANE)
+            turned = pltpu.roll(part, off, 1) if off else part
+            if off + k_pad <= LANE:
+                pieces = [(col, turned)]
+            else:
+                wide = lane_of[0:rows] >= off
+                pieces = [(col, jnp.where(wide, turned, 0.0)), (col + 1, jnp.where(wide, 0.0, turned))]
+            for c, piece in pieces:
+                cols[c] = piece if cols[c] is None else cols[c] + piece
+        for c, piece in enumerate(cols):
+            m_ref[:, c * LANE : (c + 1) * LANE] = piece.astype(BF16)
+
+    def clear():
+        stage[...] = jnp.zeros_like(stage)
+
+    for k, m_ref in enumerate(level_mats):
+        n_in, n_out = sizes[k], sizes[k + 1]
+        clear()
+        for xi in range(3):
+            row = xi * level_rows[k + 1]
+            stage[row : row + n_out, 0:n_in] = deriv_ref[xi, 0:n_out, 0:n_in]
+        lay(m_ref, level_m[k], level_k[k], stage[0 : level_m[k], :])
+    clear()
+    for xi in range(3):
+        stage[xi * NB : (xi + 1) * NB, 0:NB] = stiff_ref[xi]
+    for f in range(4):
+        row = 3 * NB + f * FR
+        stage[row : row + NF, 0:NB] = trace_ref[:, f, :]
+    lay(m_stiff, STIFF_M, 64, stage[0:STIFF_M, :])
+    lay(m_trace, 96, 64, stage[3 * NB : 3 * NB + 96, :])
+    clear()
+    for h in range(3):
+        stage[h * FR : h * FR + NF, 0:NF] = orient_ref[h]
+    lay(m_orient, 80, 32, stage[0:80, :])
+    clear()
+    for f in range(4):
+        stage[f * FR : f * FR + NF, 0:NB] = lift_ref[:, f, :]
+    lay(m_lift, 64, 96, jnp.transpose(stage[0:LANE, :])[0:64, :])
+
+    out_ref[...] = state_in[...]
+    pl.semaphore_wait(barrier, len(greeted))
+    top_start(0)
     rows = [jac_ref[xi][j : j + 1] for xi in range(3) for j in range(3)]
-    rows += [nrm_ref[f][j : j + 1] for f in range(4) for j in range(3)]
+    rows += [nrm_ref[j][f : f + 1] for f in range(4) for j in range(3)]
     rows += [mat[1:2], 2.0 * mat[2:3], mat[2:3], inv_rho]
     for t in range(TILES):
         for i, row in enumerate(rows):
@@ -154,6 +222,9 @@
         return jnp.where(rows_iota == line, 1.0, 0.0).astype(BF16)
 
     for t in range(TILES):
+        if t == 3 and n_levels > 1:
+            top_finish(0)
+            top_start(1)
         for f in range(4):
             cut = slice(t * LANE, (t + 1) * LANE)
             at = slice(f * LANE, (f + 1) * LANE)
@@ -163,14 +234,20 @@
             onehot_ghost[t, LANE : 2 * LANE, at] = g
             meta[t, 0, :, at] = jnp.broadcast_to(faces[f : f + 1, cut], (8, LANE))
             meta[t, 1, :, at] = jnp.broadcast_to(codes[f : f + 1, cut], (8, LANE))
-    sends = send_ref[...]
-    send_elem = jnp.where(sends >= 0, sends >> 2, -1)
-    send_face = sends & 3
+    send_stage[...] = jnp.zeros_like(send_stage)
+    send_lane = lax.broadcasted_iota(jnp.int32, (1, LANE), 1) // CAPC
     for c in range(3):
-        onehot_send[c] = hot(elem_rows, send_elem[c : c + 1])
-        meta_send[c] = jnp.broadcast_to(send_face[c : c + 1], (8, LANE))
-
-    pl.semaphore_wait(barrier, PEERS)
+        send_stage[c, 0:PEERS, 0:CAPC] = send_ref[c]
+    lines = []
+    for c in range(3):
+        line = send_stage[c, 0:1, :]
+        for p in range(1, PEERS):
+            turned = pltpu.roll(send_stage[c], p * CAPC, 1)[p : p + 1]
+            line = jnp.where(send_lane == p, turned, line)
+        lines.append(line)
+    for c in range(3):
+        onehot_send[c] = hot(elem_rows, jnp.where(lines[c] >= 0, lines[c] >> 2, -1))
+        meta_send[c] = jnp.broadcast_to(lines[c] & 3, (8, LANE))
 
 
     def star_rows(c, read):
@@ -229,7 +306,7 @@
             kp = level_k[k]
             m = level_m[k]
             der[0:m, :] = jnp.dot(
-                level_mats[k][...], x3[0 : 3 * kp, :], preferred_element_type=F32
+                level_mats[k][:, 0 : 3 * kp], x3[0 : 3 * kp, :], preferred_element_type=F32
             )
             n = level_rows[k + 1]
             pend = [[] for _ in range(NQ)]
@@ -281,7 +358,7 @@
                     row = (v // 2) * 16
                     tabs[idx, row : row + 16, lanes] = hi
                     tabs[idx, 512 + row : 512 + row + 16, lanes] = lo
-        der[...] = jnp.dot(m_stiff[...], x3[...], preferred_element_type=F32)
+        der[...] = jnp.dot(m_stiff[:, 0:192], x3[...], preferred_element_type=F32)
         for r in range(7):
 
             def read(xi, q, r=r):
@@ -307,7 +384,7 @@
                 [gath[512 + q * NB : 512 + (q + 1) * NB, 0:width], zero], axis=0
             ).astype(BF16)
             x = jnp.concatenate([hi, lo, hi], axis=0)
-            t = jnp.dot(m_trace[...], x, preferred_element_type=F32)
+            t = jnp.dot(m_trace[:, 0:192], x, preferred_element_type=F32)
             pick = jnp.where(
                 is_three,
                 t[3 * FR : 4 * FR],
@@ -386,10 +463,11 @@
             arrived = seen[tile, cut, :] + gath[cut, :]
             hi, lo = hi_lo(jnp.concatenate([arrived, zero], axis=0))
             x = jnp.concatenate([hi, lo, hi], axis=0)
-            t = jnp.dot(m_orient[...], x, preferred_element_type=F32)
+            t = jnp.dot(m_orient[:, 0:96], x, preferred_element_type=F32)
             seen[tile, cut, :] = jnp.where(
                 is_two, t[2 * FR : 3 * FR], jnp.where(is_one, t[FR : 2 * FR], t[0:FR])
             )
+        half_top = 0.5 * top_out[n_levels]
         lam, mu2, mu, irho = [-0.5 * coef[tile, 21 + i] for i in range(4)]
         for f in range(4):
             normal = [[coef[tile, 9 + 3 * f + j] for j in range(3)]]
@@ -417,7 +495,7 @@
                 store_split(
                     x_lift, i * 16, col, 96, fl[i * 16 : i * 16 + 16, col : col + LANE], LANE
                 )
-        der[0:64, :] = jnp.dot(m_lift[...], x_lift[...], preferred_element_type=F32)
+        der[0:64, :] = jnp.dot(m_lift[:, 0:288], x_lift[...], preferred_element_type=F32)
         for q in range(NQ):
             out_ref[q, :, lanes] = out_ref[q, :, lanes] - der[0:NB, q * LANE : (q + 1) * LANE]
 
@@ -435,7 +513,13 @@
         predict(3 + i, tables_2, w_tick)
         return carry
 
+    if n_levels > 2:
+        top_finish(1)
+        top_start(2)
     lax.fori_loop(0, 4, predict_2, 0)
+    if n_levels > 3:
+        top_finish(2)
+        top_start(3)
 
     def tick(t, carry):
         half = t // 2
@@ -507,6 +591,10 @@
 
         lax.fori_loop(0, n_due, send_step, 0)
         lax.fori_loop(0, n_tiles, gather_step, 0)
+        @pl.when(t == 0)
+        def _():
+            top_finish(n_levels - 1)
+
         lax.fori_loop(0, n_due, receive_step, 0)
         lax.fori_loop(0, n_tiles, correct_step, 0)
         return carry
@@ -530,21 +618,31 @@
     send_list,
 ):
     n_dev = lax.axis_size("dom")
-    top = jnp.max(jnp.sqrt((material[1] + 2.0 * material[2]) * (1.0 / material[0])))
-    top = lax.pmax(top, "dom").reshape(1, 1)
-    mats = prepare(deriv_mats, stiff_mats, trace_mats, lift_mats, orient_mats)
-    sends = jnp.transpose(send_list, (1, 0, 2)).reshape(3, LANE)
+    radices = []
+    while math.prod(radices) < n_dev:
+        radices.append(min(4, n_dev // math.prod(radices)))
     vmem = pl.BlockSpec(memory_space=pltpu.VMEM)
 
     def run(*refs):
-        kernel(n_dev, *refs)
+        kernel(n_dev, radices, *refs)
 
     return pl.pallas_call(
         run,
         out_shape=jax.ShapeDtypeStruct((NQ, NB, ELEMS), F32),
-        in_specs=[pl.BlockSpec(memory_space=pltpu.SMEM)] + [vmem] * 17,
+        in_specs=[vmem] * 13,
         out_specs=vmem,
         scratch_shapes=[
+            *[pltpu.VMEM((m, LANE * -(-3 * k // LANE)), BF16) for m, k in zip(level_m, level_k)],
+            pltpu.VMEM((STIFF_M, 2 * LANE), BF16),
+            pltpu.VMEM((96, 2 * LANE), BF16),
+            pltpu.VMEM((80, LANE), BF16),
+            pltpu.VMEM((64, 3 * LANE), BF16),
+            pltpu.VMEM((STIFF_M, LANE), F32),
+            pltpu.VMEM((3, 8, LANE), jnp.int32),
+            pltpu.VMEM((len(radices) + 1, 8, LANE), F32),
+            pltpu.VMEM((len(radices), 3, 8, LANE), F32),
+            pltpu.SemaphoreType.DMA((len(radices), 3)),
+            pltpu.SemaphoreType.DMA((len(radices), 3)),
             pltpu.VMEM((TILES, 25, 8, LANE), F32),
             pltpu.VMEM((7, 1024, ELEMS), BF16),
             pltpu.VMEM((TILES, ELEMS, 4 * LANE), BF16),
@@ -578,16 +676,19 @@
             flops=25_000_000_000, bytes_accessed=6_000_000, transcendentals=0
         ),
     )(
-        top,
         dof_state,
         jacobian_inv,
-        face_normals,
+        jnp.transpose(face_normals, (1, 0, 2)),
         material,
-        *mats,
+        deriv_mats,
+        stiff_mats,
+        jnp.transpose(trace_mats, (1, 0, 2)),
+        jnp.transpose(lift_mats, (2, 0, 1)),
+        orient_mats,
         nbr_slot,
         nbr_face,
         orient_code,
-        sends,
+        jnp.transpose(send_list, (1, 0, 2)),
     )
 
 

time: 176 us -> 89.7 us (0.51)
  blocking collectives: 81.4 us -> 0 us
  Pallas kernels: 75 us -> 86.7 us
  local copies, waits for them, and re-layouts: 11.2 us -> 2.83 us
  other arithmetic: 7.45 us -> 0 us
    pmax x1 -> x0, blocking collectives: 81.4 us -> none  [local(): top = lax.pmax(top, 'dom').reshape(1, 1)]
    pallas_call x1, Pallas kernels: 75 us -> 86.7 us  [local(): pl.pallas_call(run, out_shape=jax.ShapeDtypeStruct((NQ, NB, ELEMS), F32),...]
    concatenate x13 -> x0, other arithmetic: 5.78 us -> none  [the longest x8 5.66 us: split3(): return jnp.concatenate([hi, hi, lo], axis=1).astype(BF16)]
    squeeze x7 -> x0, local copies, waits for them, and re-layouts: 2.93 us -> none  [the longest x5 2.92 us: prepare(): deriv_mats[xi, :n_out, :n_in]]
    slice x3 -> x0, local copies, waits for them, and re-layouts: 2.7 us -> none  [the longest x1 0.98 us: prepare(): lift_mats[f]]
    unnamed x16 -> x1, local copies, waits for them, and re-layouts: 4.11 us -> 2.83 us
where the time goes in v1:
time: 89.7 us; the launch traced here: 89.5 us
  Pallas kernels  86.7 us (97%)
  local copies, waits for them, and re-layouts  2.83 us (3%)
    pallas_call x1, Pallas kernels, local(): pl.pallas_call(run, out_shape=jax.ShapeDtypeStruct((NQ, NB, ELEMS), F32),...  86.7 us
    unnamed x1, local copies, waits for them, and re-layouts  2.83 us

profile of v1, /device:TPU:1, one launch (start us, length us, event | category | flops | bytes accessed | tf_op | source)
XLA Modules:
  0.0 89.5 jit_solution(15766753045976103863)
XLA Ops:
  0.0 86.7 %shard_map.127 = f32[9,56,896]{2,1,0:T(8,128)} custom-call(f32[9,56,896]{2,1,0:T(8,128)} %refs_0_.1, f32[3,3,896]{2,1,0:T(4,128)} %refs_1_.1, f32[3,4,896]{2,1,0:T(4,128)} %bitcast.4, f32[3,896]{1,0:T(4,128)} %refs_3_.1, f32[3,35,56]{2,1,0:T(8,128)} %refs_4_.1, f32[3,56,56]{2,1,0:T(8,128)} %refs_5_.1, f32[21,4,56]{2,1,0:T(4,128)} %bitcast.5, ...), custom_call_target="tpu_custom_call" | custom-call | flops 24999999488 | bytes 6000000 | tf_op jit(solution)/shard_map/pallas_call | solution.py:629
  86.7 2.8 %copy.15 = f32[9,56,896]{2,1,0:T(8,128)} copy(f32[9,56,896]{2,1,0:T(8,128)} %shard_map.127) | data formatting | bytes 3612672

commit v2 on v1

--- a/solution.py
+++ b/solution.py
@@ -28,6 +28,7 @@
 STIFF_M = 272
 ROWS = NQ * FR
 PACK = 56
+SLOTS = 3
 
 
 def time_weights(lower, upper):
@@ -83,17 +84,18 @@
     meta_send,
     own,
     seen,
-    gath,
-    der,
-    x3,
+    gath_all,
+    der_all,
+    x3_all,
     lv1,
     lv2,
     lv3,
     lv4,
     lv5,
     acc,
-    fl,
-    x_lift,
+    integrals,
+    fl_all,
+    x_lift_all,
     ghost,
     sbuf,
     rbuf,
@@ -103,7 +105,7 @@
     me = lax.axis_index("dom")
     targets = [lax.rem(me + n_dev + off, n_dev) for off in peer_offsets]
     level_mats = (m0, m1, m2, m3, m4)
-    level_refs = (None, lv1, lv2, lv3, lv4, lv5)
+    levels_all = (lv1, lv2, lv3, lv4, lv5)
     partners = []
     stride = 1
     for radix in radices:
@@ -222,9 +224,6 @@
         return jnp.where(rows_iota == line, 1.0, 0.0).astype(BF16)
 
     for t in range(TILES):
-        if t == 3 and n_levels > 1:
-            top_finish(0)
-            top_start(1)
         for f in range(4):
             cut = slice(t * LANE, (t + 1) * LANE)
             at = slice(f * LANE, (f + 1) * LANE)
@@ -295,19 +294,23 @@
             pair = jnp.concatenate([pieces[i], pieces[i + 1]], axis=0)
             store_split(ref, i * 8, q * LANE, k_pad, pair, LANE)
 
-    def predict(tile, table_of, weights):
+    def predict(tile, slot, table_of, weights, keep_integral=None):
         base = pl.multiple_of(tile * LANE, LANE)
         lanes = pl.ds(base, LANE)
         cj = [[coef[tile, 3 * xi + j] for j in range(3)] for xi in range(3)]
         lam, mu2, mu, irho = [coef[tile, 21 + i] for i in range(4)]
+        x3, der = x3_all.at[slot], der_all.at[slot]
+        level_refs = [None] + [lv.at[slot] for lv in levels_all]
         for q in range(NQ):
             put_operand(x3, 64, q, [out_ref[q, r * 8 : r * 8 + 8, lanes] for r in range(7)])
+        yield
         for k in range(5):
             kp = level_k[k]
             m = level_m[k]
             der[0:m, :] = jnp.dot(
                 level_mats[k][:, 0 : 3 * kp], x3[0 : 3 * kp, :], preferred_element_type=F32
             )
+            yield
             n = level_rows[k + 1]
             pend = [[] for _ in range(NQ)]
             for r in range(n // 8):
@@ -329,6 +332,7 @@
                         store_split(x3, (r // 2) * 16, q * LANE, level_k[k + 1], pair, LANE)
                 if r % 2 == 1 or last:
                     pend = [[] for _ in range(NQ)]
+            yield
         own_pend = [[] for _ in range(NQ)]
         held = {}
         for v in range(64):
@@ -345,9 +349,12 @@
                         total = total + terms[k] * w[k]
                     ticks.append(total)
                 entries, own_int = table_of(v, ticks)
-                own_pend[q].append(own_int)
-                if r == 6:
-                    put_operand(x3, 64, q, own_pend[q])
+                if keep_integral is not None:
+                    keep_integral[v * 8 : v * 8 + 8, :] = own_int
+                else:
+                    own_pend[q].append(own_int)
+                    if r == 6:
+                        put_operand(x3, 64, q, own_pend[q])
             else:
                 entries = [(idx, jnp.zeros((8, LANE), F32)) for idx, _ in entries]
             if v % 2 == 0:
@@ -358,7 +365,24 @@
                     row = (v // 2) * 16
                     tabs[idx, row : row + 16, lanes] = hi
                     tabs[idx, 512 + row : 512 + row + 16, lanes] = lo
+        yield
+        if keep_integral is None:
+            yield from volume(tile, slot, None)
+
+    def volume(tile, slot, integral):
+        base = pl.multiple_of(tile * LANE, LANE)
+        lanes = pl.ds(base, LANE)
+        cj = [[coef[tile, 3 * xi + j] for j in range(3)] for xi in range(3)]
+        lam, mu2, mu, irho = [coef[tile, 21 + i] for i in range(4)]
+        x3, der = x3_all.at[slot], der_all.at[slot]
+        if integral is not None:
+            for q in range(NQ):
+                put_operand(
+                    x3, 64, q, [integral[(q * 7 + r) * 8 : (q * 7 + r) * 8 + 8, :] for r in range(7)]
+                )
+            yield
         der[...] = jnp.dot(m_stiff[:, 0:192], x3[...], preferred_element_type=F32)
+        yield
         for r in range(7):
 
             def read(xi, q, r=r):
@@ -371,9 +395,12 @@
                     out_ref[q, r * 8 : r * 8 + 8, lanes] - vals[q]
                 )
         own[tile] = der[168 : 168 + 96, :]
-
-    def gather_traces(table, hot_mat, face_rows, width, put):
+        yield
+
+    def gather_traces(slot, table, hot_mat, face_rows, width, put):
+        gath = gath_all.at[slot]
         gath[:, 0:width] = jnp.dot(tabs[table], hot_mat, preferred_element_type=F32)
+        yield
         is_one, is_two, is_three = [
             jnp.concatenate([face_rows == i] * 3, axis=0) for i in (1, 2, 3)
         ]
@@ -393,6 +420,14 @@
                 ),
             )
             put(q, pick)
+            yield
+
+    def together(*tasks):
+        tasks = list(tasks)
+        while tasks:
+            for task in list(tasks):
+                if next(task, "end") == "end":
+                    tasks.remove(task)
 
     lane_group = lax.broadcasted_iota(jnp.int32, (PACK, LANE), 1) // CAPC
 
@@ -421,24 +456,26 @@
             for p in range(PEERS)
         ]
 
-    def send_cluster(c, combo):
+    def send_cluster(c, combo, slot):
+        staged = fl_all.at[slot, 0 : 4 * PACK, 0:LANE]
+
         def put(q, pick):
-            ghost_stage[q * FR : (q + 1) * FR, :] = pick
-
-        ghost_stage = fl.at[0 : 4 * PACK, 0:LANE]
-        ghost_stage[ROWS : 4 * PACK, :] = jnp.zeros((4 * PACK - ROWS, LANE), F32)
-        gather_traces(combo, onehot_send[c], meta_send[c], LANE, put)
-        outs = transpose_blocks(lambda g: ghost_stage[g * PACK : (g + 1) * PACK, :])
+            staged[q * FR : (q + 1) * FR, :] = pick
+
+        staged[ROWS : 4 * PACK, :] = jnp.zeros((4 * PACK - ROWS, LANE), F32)
+        yield from gather_traces(slot, combo, onehot_send[c], meta_send[c], LANE, put)
+        outs = transpose_blocks(lambda g: staged[g * PACK : (g + 1) * PACK, :])
         for p in range(PEERS):
             sbuf[combo, p] = outs[p]
         for copy in copies(combo):
             copy.start()
-
-    def gather_tile(tile, table):
+        yield
+
+    def gather_tile(tile, table, slot):
         def put(q, pick):
             seen[tile, q * FR : (q + 1) * FR, :] = pick
 
-        gather_traces(table, onehot[tile], meta[tile, 0], 4 * LANE, put)
+        yield from gather_traces(slot, table, onehot[tile], meta[tile, 0], 4 * LANE, put)
 
     def receive_cluster(c, combo):
         for copy in copies(combo):
@@ -449,12 +486,14 @@
         ghost[c, :, 0:LANE] = hi
         ghost[c, :, LANE : 2 * LANE] = lo
 
-    def correct_tile(tile, c):
+    def correct_tile(tile, c, slot):
         base = pl.multiple_of(tile * LANE, LANE)
         lanes = pl.ds(base, LANE)
+        gath, fl, x_lift, der = gath_all.at[slot], fl_all.at[slot], x_lift_all.at[slot], der_all.at[slot]
         gath[0 : 4 * PACK, :] = jnp.dot(
             ghost[c], onehot_ghost[tile], preferred_element_type=F32
         )
+        yield
         code = meta[tile, 1]
         is_one, is_two = [jnp.concatenate([code == i] * 3, axis=0) for i in (1, 2)]
         zero = jnp.zeros((8, 4 * LANE), F32)
@@ -464,9 +503,10 @@
             hi, lo = hi_lo(jnp.concatenate([arrived, zero], axis=0))
             x = jnp.concatenate([hi, lo, hi], axis=0)
             t = jnp.dot(m_orient[:, 0:96], x, preferred_element_type=F32)
-            seen[tile, cut, :] = jnp.where(
+            gath[512 + q * FR : 512 + (q + 1) * FR, :] = jnp.where(
                 is_two, t[2 * FR : 3 * FR], jnp.where(is_one, t[FR : 2 * FR], t[0:FR])
             )
+            yield
         half_top = 0.5 * top_out[n_levels]
         lam, mu2, mu, irho = [-0.5 * coef[tile, 21 + i] for i in range(4)]
         for f in range(4):
@@ -477,8 +517,9 @@
                     for q in range(NQ)
                 ]
                 outer = [
-                    seen[
-                        tile, q * FR + r * 8 : q * FR + r * 8 + 8, f * LANE : (f + 1) * LANE
+                    gath[
+                        512 + q * FR + r * 8 : 512 + q * FR + r * 8 + 8,
+                        f * LANE : (f + 1) * LANE,
                     ]
                     for q in range(NQ)
                 ]
@@ -489,15 +530,19 @@
                     fl[row : row + 8, q * LANE : (q + 1) * LANE] = vals[q] + half_top * (
                         inner[q] - outer[q]
                     )
-        for i in range(6):
-            for q in range(NQ):
-                col = q * LANE
-                store_split(
-                    x_lift, i * 16, col, 96, fl[i * 16 : i * 16 + 16, col : col + LANE], LANE
-                )
+            if f % 2:
+                for i in range(3 * (f // 2), 3 * (f // 2) + 3):
+                    for q in range(NQ):
+                        col = q * LANE
+                        store_split(
+                            x_lift, i * 16, col, 96, fl[i * 16 : i * 16 + 16, col : col + LANE], LANE
+                        )
+            yield
         der[0:64, :] = jnp.dot(m_lift[:, 0:288], x_lift[...], preferred_element_type=F32)
+        yield
         for q in range(NQ):
             out_ref[q, :, lanes] = out_ref[q, :, lanes] - der[0:NB, q * LANE : (q + 1) * LANE]
+        yield
 
 
     acc[...] = jnp.zeros_like(acc)
@@ -513,93 +558,113 @@
         predict(3 + i, tables_2, w_tick)
         return carry
 
-    if n_levels > 2:
-        top_finish(1)
-        top_start(2)
-    lax.fori_loop(0, 4, predict_2, 0)
-    if n_levels > 3:
-        top_finish(2)
-        top_start(3)
-
-    def tick(t, carry):
-        half = t // 2
-        odd = t - 2 * half
-        last = t // 3
-
-        @pl.when(odd == 0)
+    def advance(level):
+        if level < n_levels:
+            top_finish(level)
+            if level + 1 < n_levels:
+                top_start(level + 1)
+
+    def predict_2(i, carry):
+        @pl.when(i == 1)
         def _():
-            def tables_1(v, ticks):
+            advance(0)
+
+        together(
+            *[
+                predict(3 + 2 * i + n, n, tables_2, w_tick, integrals.at[2 * i + n])
+                for n in range(2)
+            ]
+        )
+        return carry
+
+    lax.fori_loop(0, 2, predict_2, 0)
+    advance(1)
+
+    def two_ticks(half, carry):
+        even = 2 * half
+        odd = even + 1
+
+        def tables_1(n):
+            def inner(v, ticks):
                 j0, j1 = ticks
                 pair = j0 + j1
-                return [(t, j0), (t + 1, j1), (4 + half, pair)], pair
-
-            def tables_1_all(i):
-                def inner(v, ticks):
-                    entries, pair = tables_1(v, ticks)
-                    whole = pair + acc[2 + i, v * 8 : v * 8 + 8, :]
-                    acc[2 + i, v * 8 : v * 8 + 8, :] = whole
-                    return entries + [(6, whole)], pair
-
-                return inner
-
-            def predict_1(i, carry):
-                predict(1 + i, tables_1_all(i), w_tick[:2])
-                return carry
-
-            lax.fori_loop(0, 2, predict_1, 0)
-
-        keep = (1 - odd).astype(F32)
-
-        def tables_0(v, ticks):
+                rows_v = slice(v * 8, v * 8 + 8)
+                whole = pair + acc[2 + n, rows_v, :]
+                acc[2 + n, rows_v, :] = whole
+                return [(even, j0), (odd, j1), (4 + half, pair), (6, whole)], pair
+
+            return inner
+
+        def tables_0_even(v, ticks):
+            (j0,) = ticks
+            acc[0, v * 8 : v * 8 + 8, :] = j0
+            return [(even, j0)], j0
+
+        def tables_0_odd(v, ticks):
             (j0,) = ticks
             rows_v = slice(v * 8, v * 8 + 8)
             pair = j0 + acc[0, rows_v, :]
-            acc[0, rows_v, :] = pair * keep
-            whole = j0 + acc[1, rows_v, :]
+            whole = pair + acc[1, rows_v, :]
             acc[1, rows_v, :] = whole
-            return [(t, j0), (4 + half, pair), (6, whole)], j0
-
-        predict(0, tables_0, w_tick[:1])
-
-        n_due = 1 + odd + last
-        n_tiles = 1 + 2 * odd + 4 * last
-
-        def combo_of(a, b):
-            return (1 - a) * t + (a - b) * (4 + half) + b * 6
-
-        def send_step(c, carry):
-            a = (c + 1) // 2
-            b = c // 2
-            send_cluster(c, combo_of(a, b))
+            return [(odd, j0), (4 + half, pair), (6, whole)], j0
+
+        together(
+            predict(0, 0, tables_0_even, w_tick[:1]),
+            predict(1, 1, tables_1(0), w_tick[:2]),
+            predict(2, 2, tables_1(1), w_tick[:2]),
+        )
+
+        @pl.when(half == 0)
+        def _():
+            advance(2)
+
+        together(send_cluster(0, even, 0))
+        together(
+            gather_tile(0, even, 1),
+            volume(3 + 2 * half, 0, integrals.at[2 * half]),
+            volume(4 + 2 * half, 2, integrals.at[2 * half + 1]),
+        )
+
+        @pl.when(half == 0)
+        def _():
+            advance(3)
+
+        receive_cluster(0, even)
+        together(correct_tile(0, 0, 0))
+
+        together(predict(0, 0, tables_0_odd, w_tick[:1]))
+        together(send_cluster(0, odd, 0), send_cluster(1, 4 + half, 1))
+
+        @pl.when(half == 1)
+        def _():
+            together(send_cluster(2, 6, 2))
+
+        together(gather_tile(0, odd, 0), gather_tile(1, 4 + half, 1), gather_tile(2, 4 + half, 2))
+
+        def gather_2(i, carry):
+            together(*[gather_tile(3 + 2 * i + n, 6, n) for n in range(2)])
             return carry
 
-        def gather_step(j, carry):
-            a = (j + 6) // 7
-            b = (j + 4) // 7
-            gather_tile(j, combo_of(a, b))
+        @pl.when(half == 1)
+        def _():
+            lax.fori_loop(0, 2, gather_2, 0)
+
+        receive_cluster(0, odd)
+        receive_cluster(1, 4 + half)
+        together(correct_tile(0, 0, 0), correct_tile(1, 1, 1), correct_tile(2, 1, 2))
+
+        def correct_2(i, carry):
+            together(*[correct_tile(3 + 2 * i + n, 2, n) for n in range(2)])
             return carry
 
-        def receive_step(c, carry):
-            a = (c + 1) // 2
-            b = c // 2
-            receive_cluster(c, combo_of(a, b))
-            return carry
-
-        def correct_step(j, carry):
-            correct_tile(j, (j + 6) // 7 + (j + 4) // 7)
-            return carry
-
-        lax.fori_loop(0, n_due, send_step, 0)
-        lax.fori_loop(0, n_tiles, gather_step, 0)
-        @pl.when(t == 0)
+        @pl.when(half == 1)
         def _():
-            top_finish(n_levels - 1)
-
-        lax.fori_loop(0, n_due, receive_step, 0)
-        lax.fori_loop(0, n_tiles, correct_step, 0)
+            receive_cluster(2, 6)
+            lax.fori_loop(0, 2, correct_2, 0)
+
         return carry
 
-    lax.fori_loop(0, 4, tick, 0)
+    lax.fori_loop(0, 2, two_ticks, 0)
 
 
 def local(
@@ -652,17 +717,18 @@
             pltpu.VMEM((3, 8, LANE), jnp.int32),
             pltpu.VMEM((TILES, 96, NQ * LANE), F32),
             pltpu.VMEM((TILES, ROWS, 4 * LANE), F32),
-            pltpu.VMEM((1024, 4 * LANE), F32),
-            pltpu.VMEM((STIFF_M, NQ * LANE), F32),
-            pltpu.VMEM((192, NQ * LANE), BF16),
-            pltpu.VMEM((NQ, 40, LANE), F32),
-            pltpu.VMEM((NQ, 24, LANE), F32),
-            pltpu.VMEM((NQ, 16, LANE), F32),
-            pltpu.VMEM((NQ, 8, LANE), F32),
-            pltpu.VMEM((NQ, 8, LANE), F32),
+            pltpu.VMEM((SLOTS, 1024, 4 * LANE), F32),
+            pltpu.VMEM((SLOTS, STIFF_M, NQ * LANE), F32),
+            pltpu.VMEM((SLOTS, 192, NQ * LANE), BF16),
+            pltpu.VMEM((SLOTS, NQ, 40, LANE), F32),
+            pltpu.VMEM((SLOTS, NQ, 24, LANE), F32),
+            pltpu.VMEM((SLOTS, NQ, 16, LANE), F32),
+            pltpu.VMEM((SLOTS, NQ, 8, LANE), F32),
+            pltpu.VMEM((SLOTS, NQ, 8, LANE), F32),
             pltpu.VMEM((4, NQ * NB, LANE), F32),
-            pltpu.VMEM((4 * PACK, NQ * LANE), F32),
-            pltpu.VMEM((288, NQ * LANE), BF16),
+            pltpu.VMEM((4, NQ * NB, LANE), F32),
+            pltpu.VMEM((SLOTS, 4 * PACK, NQ * LANE), F32),
+            pltpu.VMEM((SLOTS, 288, NQ * LANE), BF16),
             pltpu.VMEM((3, 4 * PACK, 2 * LANE), BF16),
             pltpu.VMEM((7, PEERS, PACK, LANE), F32),
             pltpu.VMEM((7, PEERS, PACK, LANE), F32),

time: 89.7 us -> 79.9 us (0.89)
  Pallas kernels: 86.7 us -> 77 us
    pallas_call x1, Pallas kernels: 86.7 us -> 77 us  [local(): pl.pallas_call(run, out_shape=jax.ShapeDtypeStruct((NQ, NB, ELEMS), F32),...]
where the time goes in v2:
time: 79.9 us; the launch traced here: 79.8 us
  Pallas kernels  77 us (96%)
  local copies, waits for them, and re-layouts  2.83 us (4%)
    pallas_call x1, Pallas kernels, local(): pl.pallas_call(run, out_shape=jax.ShapeDtypeStruct((NQ, NB, ELEMS), F32),...  77 us
    unnamed x1, local copies, waits for them, and re-layouts  2.83 us

profile of v2, /device:TPU:1, one launch (start us, length us, event | category | flops | bytes accessed | tf_op | source)
XLA Modules:
  0.0 79.8 jit_solution(7998727489688924904)
XLA Ops:
  0.0 77.0 %shard_map.127 = f32[9,56,896]{2,1,0:T(8,128)} custom-call(f32[9,56,896]{2,1,0:T(8,128)} %refs_0_.1, f32[3,3,896]{2,1,0:T(4,128)} %refs_1_.1, f32[3,4,896]{2,1,0:T(4,128)} %bitcast.4, f32[3,896]{1,0:T(4,128)} %refs_3_.1, f32[3,35,56]{2,1,0:T(8,128)} %refs_4_.1, f32[3,56,56]{2,1,0:T(8,128)} %refs_5_.1, f32[21,4,56]{2,1,0:T(4,128)} %bitcast.5, ...), custom_call_target="tpu_custom_call" | custom-call | flops 24999999488 | bytes 6000000 | tf_op jit(solution)/shard_map/pallas_call | solution.py:694
  77.0 2.8 %copy.15 = f32[9,56,896]{2,1,0:T(8,128)} copy(f32[9,56,896]{2,1,0:T(8,128)} %shard_map.127) | data formatting | bytes 3612672

commit v3 on v2

--- a/solution.py
+++ b/solution.py
@@ -75,6 +75,7 @@
     top_in,
     top_send_sem,
     top_recv_sem,
+    state_sem,
     coef,
     tabs,
     onehot,
@@ -119,6 +120,8 @@
     for dev in greeted:
         pl.semaphore_signal(barrier, inc=1, device_id=(dev,), device_id_type=pl.DeviceIdType.MESH)
 
+    state_copy = pltpu.make_async_copy(state_in, out_ref, state_sem)
+    state_copy.start()
     mat = mat_ref[...]
     inv_rho = 1.0 / mat[0:1]
     speed = jnp.sqrt((mat[1:2] + 2.0 * mat[2:3]) * inv_rho)
@@ -197,9 +200,7 @@
         stage[f * FR : f * FR + NF, 0:NB] = lift_ref[:, f, :]
     lay(m_lift, 64, 96, jnp.transpose(stage[0:LANE, :])[0:64, :])
 
-    out_ref[...] = state_in[...]
-    pl.semaphore_wait(barrier, len(greeted))
-    top_start(0)
+    state_copy.wait()
     rows = [jac_ref[xi][j : j + 1] for xi in range(3) for j in range(3)]
     rows += [nrm_ref[j][f : f + 1] for f in range(4) for j in range(3)]
     rows += [mat[1:2], 2.0 * mat[2:3], mat[2:3], inv_rho]
@@ -223,16 +224,19 @@
     def hot(rows_iota, line):
         return jnp.where(rows_iota == line, 1.0, 0.0).astype(BF16)
 
-    for t in range(TILES):
-        for f in range(4):
-            cut = slice(t * LANE, (t + 1) * LANE)
-            at = slice(f * LANE, (f + 1) * LANE)
-            onehot[t, :, at] = hot(elem_rows, slots[f : f + 1, cut])
-            g = hot(ghost_rows, ghost_col[f : f + 1, cut])
-            onehot_ghost[t, 0:LANE, at] = g
-            onehot_ghost[t, LANE : 2 * LANE, at] = g
-            meta[t, 0, :, at] = jnp.broadcast_to(faces[f : f + 1, cut], (8, LANE))
-            meta[t, 1, :, at] = jnp.broadcast_to(codes[f : f + 1, cut], (8, LANE))
+    def build_onehots(tiles):
+        for t in tiles:
+            for f in range(4):
+                cut = slice(t * LANE, (t + 1) * LANE)
+                at = slice(f * LANE, (f + 1) * LANE)
+                onehot[t, :, at] = hot(elem_rows, slots[f : f + 1, cut])
+                g = hot(ghost_rows, ghost_col[f : f + 1, cut])
+                onehot_ghost[t, 0:LANE, at] = g
+                onehot_ghost[t, LANE : 2 * LANE, at] = g
+                meta[t, 0, :, at] = jnp.broadcast_to(faces[f : f + 1, cut], (8, LANE))
+                meta[t, 1, :, at] = jnp.broadcast_to(codes[f : f + 1, cut], (8, LANE))
+
+    build_onehots([0])
     send_stage[...] = jnp.zeros_like(send_stage)
     send_lane = lax.broadcasted_iota(jnp.int32, (1, LANE), 1) // CAPC
     for c in range(3):
@@ -459,11 +463,27 @@
     def send_cluster(c, combo, slot):
         staged = fl_all.at[slot, 0 : 4 * PACK, 0:LANE]
 
-        def put(q, pick):
-            staged[q * FR : (q + 1) * FR, :] = pick
-
         staged[ROWS : 4 * PACK, :] = jnp.zeros((4 * PACK - ROWS, LANE), F32)
-        yield from gather_traces(slot, combo, onehot_send[c], meta_send[c], LANE, put)
+        gath, x3, der = gath_all.at[slot], x3_all.at[slot], der_all.at[slot]
+        gath[:, 0:LANE] = jnp.dot(tabs[combo], onehot_send[c], preferred_element_type=F32)
+        yield
+        zero = jnp.zeros((8, LANE), F32)
+        for q in range(NQ):
+            hi, lo = [
+                jnp.concatenate([gath[row : row + NB, 0:LANE], zero], axis=0).astype(BF16)
+                for row in (q * NB, 512 + q * NB)
+            ]
+            for i, part in enumerate((hi, lo, hi)):
+                x3[64 * i : 64 * i + 64, q * LANE : (q + 1) * LANE] = part
+        der[0:96, :] = jnp.dot(m_trace[:, 0:192], x3[...], preferred_element_type=F32)
+        yield
+        picks = [jnp.concatenate([meta_send[c] == i] * 3, axis=0) for i in (1, 2, 3)]
+        for q in range(NQ):
+            best = der[0:FR, q * LANE : (q + 1) * LANE]
+            for i, pick in enumerate(picks):
+                row = (i + 1) * FR
+                best = jnp.where(pick, der[row : row + FR, q * LANE : (q + 1) * LANE], best)
+            staged[q * FR : (q + 1) * FR, :] = best
         outs = transpose_blocks(lambda g: staged[g * PACK : (g + 1) * PACK, :])
         for p in range(PEERS):
             sbuf[combo, p] = outs[p]
@@ -554,31 +574,22 @@
         whole = first + second
         return [(0, j0), (1, j1), (2, j2), (3, j3), (4, first), (5, second), (6, whole)], whole
 
-    def predict_2(i, carry):
-        predict(3 + i, tables_2, w_tick)
-        return carry
-
     def advance(level):
         if level < n_levels:
             top_finish(level)
             if level + 1 < n_levels:
                 top_start(level + 1)
 
-    def predict_2(i, carry):
-        @pl.when(i == 1)
-        def _():
-            advance(0)
-
+    def predict_2(first):
         together(
-            *[
-                predict(3 + 2 * i + n, n, tables_2, w_tick, integrals.at[2 * i + n])
-                for n in range(2)
-            ]
+            *[predict(3 + n, n - first, tables_2, w_tick, integrals.at[n]) for n in (first, first + 1)]
         )
-        return carry
-
-    lax.fori_loop(0, 2, predict_2, 0)
-    advance(1)
+
+    predict_2(0)
+    pl.semaphore_wait(barrier, len(greeted))
+    top_start(0)
+    predict_2(2)
+    advance(0)
 
     def two_ticks(half, carry):
         even = 2 * half
@@ -609,20 +620,31 @@
             return [(odd, j0), (4 + half, pair), (6, whole)], j0
 
         together(
-            predict(0, 0, tables_0_even, w_tick[:1]),
-            predict(1, 1, tables_1(0), w_tick[:2]),
-            predict(2, 2, tables_1(1), w_tick[:2]),
+            predict(0, 0, tables_0_even, w_tick[:1], integrals.at[4]),
+            predict(1, 1, tables_1(0), w_tick[:2], integrals.at[5]),
+            predict(2, 2, tables_1(1), w_tick[:2], integrals.at[6]),
         )
+
+        @pl.when(half == 0)
+        def _():
+            advance(1)
+
+        together(send_cluster(0, even, 0))
 
         @pl.when(half == 0)
         def _():
             advance(2)
-
-        together(send_cluster(0, even, 0))
+            build_onehots(range(1, TILES))
+
         together(
             gather_tile(0, even, 1),
+            volume(0, 0, integrals.at[4]),
+            volume(1, 1, integrals.at[5]),
+            volume(2, 2, integrals.at[6]),
+        )
+        together(
             volume(3 + 2 * half, 0, integrals.at[2 * half]),
-            volume(4 + 2 * half, 2, integrals.at[2 * half + 1]),
+            volume(4 + 2 * half, 1, integrals.at[2 * half + 1]),
         )
 
         @pl.when(half == 0)
@@ -632,14 +654,19 @@
         receive_cluster(0, even)
         together(correct_tile(0, 0, 0))
 
-        together(predict(0, 0, tables_0_odd, w_tick[:1]))
+        together(predict(0, 0, tables_0_odd, w_tick[:1], integrals.at[4]))
         together(send_cluster(0, odd, 0), send_cluster(1, 4 + half, 1))
 
         @pl.when(half == 1)
         def _():
             together(send_cluster(2, 6, 2))
 
-        together(gather_tile(0, odd, 0), gather_tile(1, 4 + half, 1), gather_tile(2, 4 + half, 2))
+        together(
+            gather_tile(0, odd, 0),
+            volume(0, 0, integrals.at[4]),
+            gather_tile(1, 4 + half, 1),
+            gather_tile(2, 4 + half, 2),
+        )
 
         def gather_2(i, carry):
             together(*[gather_tile(3 + 2 * i + n, 6, n) for n in range(2)])
@@ -694,7 +721,7 @@
     return pl.pallas_call(
         run,
         out_shape=jax.ShapeDtypeStruct((NQ, NB, ELEMS), F32),
-        in_specs=[vmem] * 13,
+        in_specs=[pl.BlockSpec(memory_space=pl.ANY)] + [vmem] * 12,
         out_specs=vmem,
         scratch_shapes=[
             *[pltpu.VMEM((m, LANE * -(-3 * k // LANE)), BF16) for m, k in zip(level_m, level_k)],
@@ -708,6 +735,7 @@
             pltpu.VMEM((len(radices), 3, 8, LANE), F32),
             pltpu.SemaphoreType.DMA((len(radices), 3)),
             pltpu.SemaphoreType.DMA((len(radices), 3)),
+            pltpu.SemaphoreType.DMA,
             pltpu.VMEM((TILES, 25, 8, LANE), F32),
             pltpu.VMEM((7, 1024, ELEMS), BF16),
             pltpu.VMEM((TILES, ELEMS, 4 * LANE), BF16),
@@ -726,7 +754,7 @@
             pltpu.VMEM((SLOTS, NQ, 8, LANE), F32),
             pltpu.VMEM((SLOTS, NQ, 8, LANE), F32),
             pltpu.VMEM((4, NQ * NB, LANE), F32),
-            pltpu.VMEM((4, NQ * NB, LANE), F32),
+            pltpu.VMEM((7, NQ * NB, LANE), F32),
             pltpu.VMEM((SLOTS, 4 * PACK, NQ * LANE), F32),
             pltpu.VMEM((SLOTS, 288, NQ * LANE), BF16),
             pltpu.VMEM((3, 4 * PACK, 2 * LANE), BF16),

time: 79.9 us -> 74 us (0.926)
  Pallas kernels: 77 us -> 71 us
    pallas_call x1, Pallas kernels: 77 us -> 71 us  [local(): pl.pallas_call(run, out_shape=jax.ShapeDtypeStruct((NQ, NB, ELEMS), F32),...]
where the time goes in v3:
time: 74 us; the launch traced here: 73.8 us
  Pallas kernels  71 us (96%)
  local copies, waits for them, and re-layouts  2.83 us (4%)
    pallas_call x1, Pallas kernels, local(): pl.pallas_call(run, out_shape=jax.ShapeDtypeStruct((NQ, NB, ELEMS), F32),...  71 us
    unnamed x1, local copies, waits for them, and re-layouts  2.83 us

profile of v3, /device:TPU:1, one launch (start us, length us, event | category | flops | bytes accessed | tf_op | source)
XLA Modules:
  0.0 73.8 jit_solution(4158609918332915404)
XLA Ops:
  0.0 71.0 %shard_map.127 = f32[9,56,896]{2,1,0:T(8,128)} custom-call(f32[9,56,896]{2,1,0:T(8,128)} %refs_0_.1, f32[3,3,896]{2,1,0:T(4,128)} %refs_1_.1, f32[3,4,896]{2,1,0:T(4,128)} %bitcast.4, f32[3,896]{1,0:T(4,128)} %refs_3_.1, f32[3,35,56]{2,1,0:T(8,128)} %refs_4_.1, f32[3,56,56]{2,1,0:T(8,128)} %refs_5_.1, f32[21,4,56]{2,1,0:T(4,128)} %bitcast.5, ...), custom_call_target="tpu_custom_call" | custom-call | flops 24999999488 | bytes 6000000 | tf_op jit(solution)/shard_map/pallas_call | solution.py:721
  71.0 2.8 %copy.15 = f32[9,56,896]{2,1,0:T(8,128)} copy(f32[9,56,896]{2,1,0:T(8,128)} %shard_map.127) | data formatting | bytes 3612672

commit v4 on v3

--- a/solution.py
+++ b/solution.py
@@ -642,10 +642,9 @@
             volume(1, 1, integrals.at[5]),
             volume(2, 2, integrals.at[6]),
         )
-        together(
-            volume(3 + 2 * half, 0, integrals.at[2 * half]),
-            volume(4 + 2 * half, 1, integrals.at[2 * half + 1]),
-        )
+        @pl.when(half == 1)
+        def _():
+            together(volume(5, 0, integrals.at[2]), volume(6, 1, integrals.at[3]))
 
         @pl.when(half == 0)
         def _():
@@ -660,6 +659,10 @@
         @pl.when(half == 1)
         def _():
             together(send_cluster(2, 6, 2))
+
+        @pl.when(half == 0)
+        def _():
+            together(volume(3, 0, integrals.at[0]), volume(4, 1, integrals.at[1]))
 
         together(
             gather_tile(0, odd, 0),
@@ -668,26 +671,20 @@
             gather_tile(2, 4 + half, 2),
         )
 
-        def gather_2(i, carry):
-            together(*[gather_tile(3 + 2 * i + n, 6, n) for n in range(2)])
-            return carry
-
         @pl.when(half == 1)
         def _():
-            lax.fori_loop(0, 2, gather_2, 0)
+            together(*[gather_tile(3 + n, 6, n) for n in range(2)])
+            together(*[gather_tile(5 + n, 6, n) for n in range(2)])
 
         receive_cluster(0, odd)
         receive_cluster(1, 4 + half)
         together(correct_tile(0, 0, 0), correct_tile(1, 1, 1), correct_tile(2, 1, 2))
 
-        def correct_2(i, carry):
-            together(*[correct_tile(3 + 2 * i + n, 2, n) for n in range(2)])
-            return carry
-
         @pl.when(half == 1)
         def _():
             receive_cluster(2, 6)
-            lax.fori_loop(0, 2, correct_2, 0)
+            together(*[correct_tile(3 + n, 2, n) for n in range(2)])
+            together(*[correct_tile(5 + n, 2, n) for n in range(2)])
 
         return carry
 

time: 74 us -> 73.4 us (level)
  no operation moved by 1% of the time
where the time goes in v4:
time: 73.4 us; the launch traced here: 73.3 us
  Pallas kernels  70.4 us (96%)
  local copies, waits for them, and re-layouts  2.83 us (4%)
    pallas_call x1, Pallas kernels, local(): pl.pallas_call(run, out_shape=jax.ShapeDtypeStruct((NQ, NB, ELEMS), F32),...  70.4 us
    unnamed x1, local copies, waits for them, and re-layouts  2.83 us

profile of v4, /device:TPU:1, one launch (start us, length us, event | category | flops | bytes accessed | tf_op | source)
XLA Modules:
  0.0 73.3 jit_solution(1571084348980653861)
XLA Ops:
  0.0 70.4 %shard_map.127 = f32[9,56,896]{2,1,0:T(8,128)} custom-call(f32[9,56,896]{2,1,0:T(8,128)} %refs_0_.1, f32[3,3,896]{2,1,0:T(4,128)} %refs_1_.1, f32[3,4,896]{2,1,0:T(4,128)} %bitcast.4, f32[3,896]{1,0:T(4,128)} %refs_3_.1, f32[3,35,56]{2,1,0:T(8,128)} %refs_4_.1, f32[3,56,56]{2,1,0:T(8,128)} %refs_5_.1, f32[21,4,56]{2,1,0:T(4,128)} %bitcast.5, ...), custom_call_target="tpu_custom_call" | custom-call | flops 24999999488 | bytes 6000000 | tf_op jit(solution)/shard_map/pallas_call | solution.py:718
  70.4 2.8 %copy.15 = f32[9,56,896]{2,1,0:T(8,128)} copy(f32[9,56,896]{2,1,0:T(8,128)} %shard_map.127) | data formatting | bytes 3612672
